TPU v7x, 256 devices: a whole 4x4x8 slice. The times are simulated.
256 devices in a mesh: dp: 32 (over y, z), mp: 8 (over x, core).
Axes of the slice: x: 4, y: 4, z: 8, core: 2. Of those that a mesh axis runs over, the one named last changes fastest.
Arguments:
- gradient: bfloat16 [8, 96, 512, 512], P('mp', None, 'dp'), may hold values from -60 to 60
- owner_order: int32 [96], replicated, may hold values from 0 to 95, each once
- left_factor: bfloat16 [8, 96, 512, 512], P('mp', 'dp'), may hold values from -1 to 2, as said below
- right_factor: bfloat16 [8, 96, 512, 512], P('mp', 'dp'), may hold values from -1 to 2, as said below
- left_root: bfloat16 [8, 96, 512, 512], P('mp', 'dp'), may hold values from -1 to 2.5, as said below
- right_root: bfloat16 [8, 96, 512, 512], P('mp', 'dp'), may hold values from -1 to 2.5, as said below
Outputs:
- update: bfloat16 [8, 96, 512, 512], P('mp', None, 'dp')
- left_next: bfloat16 [8, 96, 512, 512], P('mp', 'dp')
- right_next: bfloat16 [8, 96, 512, 512], P('mp', 'dp')
Inputs may be any that keep to these rules, and one draw needn't show every extreme that they name: `owner_order`: the block in slot p is owned by data index p // 3. `left_factor`: symmetric. `right_factor`: symmetric. `left_root`: symmetric. `right_root`: symmetric.
All inputs are finite; a program needn't handle non-finite values.
Results may differ from a plain program's by a relative error of at most 0.0049.
Values may be sent and summed in bfloat16 or wider, within the bound.
A program may use at most 64 MiB of HBM per device.

v0:
```python
import jax
import jax.numpy as jnp
from jax import lax
from jax.sharding import PartitionSpec as P

factor_decay = 0.9
epsilon = 1e-06


def local_blocks(grad_block, left_old, right_old, left_inv, right_inv):
    block_size = grad_block.shape[-1]
    gram_left = jnp.einsum(
        "kij,kmj->kim", grad_block, grad_block, preferred_element_type=jnp.float32
    )
    gram_right = jnp.einsum(
        "kji,kjm->kim", grad_block, grad_block, preferred_element_type=jnp.float32
    )
    coef = (1.0 - factor_decay) / block_size
    left_new = (factor_decay * left_old.astype(jnp.float32) + coef * gram_left).astype(jnp.bfloat16)
    right_new = (factor_decay * right_old.astype(jnp.float32) + coef * gram_right).astype(
        jnp.bfloat16
    )
    left_applied = jnp.einsum(
        "kij,kjm->kim", left_inv, grad_block, preferred_element_type=jnp.float32
    ).astype(jnp.bfloat16)
    conditioned = jnp.einsum(
        "kij,kjm->kim", left_applied, right_inv, preferred_element_type=jnp.float32
    )
    grad_square = jnp.sum(jnp.square(grad_block.astype(jnp.float32)), axis=(1, 2))
    cond_square = jnp.sum(conditioned * conditioned, axis=(1, 2))
    return (left_new, right_new, conditioned, grad_square, cond_square)


def grafted(conditioned, grad_total, cond_total):
    graft = jnp.sqrt((grad_total + epsilon) / (cond_total + epsilon))
    return (-graft[:, None, None] * conditioned).astype(jnp.bfloat16)


def body(gradient, owner_order, left_factor, right_factor, left_root, right_root):
    blocks = gradient.shape[1]
    ordered = jnp.take(gradient, owner_order, axis=1)
    owned = lax.all_to_all(ordered, "dp", split_axis=1, concat_axis=2, tiled=True)[0]
    left_new, right_new, conditioned, grad_square, cond_square = local_blocks(
        owned, left_factor[0], right_factor[0], left_root[0], right_root[0]
    )
    grad_total, cond_total = lax.psum((grad_square, cond_square), "mp")
    update_slot = grafted(conditioned, grad_total, cond_total)
    returned = lax.all_to_all(update_slot[None], "dp", split_axis=2, concat_axis=1, tiled=True)
    left_next = left_new[None]
    right_next = right_new[None]
    places = (
        jnp.zeros((blocks,), jnp.int32).at[owner_order].set(jnp.arange(blocks, dtype=jnp.int32))
    )
    update = jnp.take(returned, places, axis=1)
    return (update, left_next, right_next)


def solution(mesh):
    return jax.shard_map(
        body,
        mesh=mesh,
        in_specs=(
            P("mp", None, "dp", None),
            P(),
            P("mp", "dp", None, None),
            P("mp", "dp", None, None),
            P("mp", "dp", None, None),
            P("mp", "dp", None, None),
        ),
        out_specs=(P("mp", None, "dp", None), P("mp", "dp", None, None), P("mp", "dp", None, None)),
        check_vma=False,
    )
```

profile of v0, /device:TPU:40, one launch (start us, length us, event | category | flops | bytes accessed | tf_op | source)
XLA Modules:
  0.0 139.6 jit_solution(6405584692164068193)
XLA Ops:
  0.6 0.0 copy-start
  0.6 0.8 compare_select_fusion.1
  1.4 0.7 compare_and_fusion.1
  2.1 0.0 copy-done
  2.1 0.7 gather_fusion
  2.8 0.2 bitcast_select_fusion.1
  3.0 50.3 %all_to_all.33 = bf16[1,96,16,512]{3,2,0,1:T(8,128)(2,1)S(1)} all-to-all(bf16[1,96,16,512]{3,2,0,1:T(8,128)(2,1)S(1)} %bitcast_select_fusion.1), channel_id=1, replica_groups=mesh['dp'=32,'mp'=8] {'dp'}, dimensions={1} | all-to-all | bytes 3145728 | tf_op jit(solution)/shard_map/all_to_all | solution.py:42
  53.3 0.1 copy.26
  53.5 0.5 multiply_reduce_fusion.1
  54.0 5.5 %multiply_reduce_fusion = (f32[3]{0:T(128)S(1)}, f32[3,512,512]{2,1,0:T(8,128)}) fusion(bf16[1,3,512,512]{3,2,1,0:T(8,128)(2,1)} %param.13, bf16[3,512,512]{2,1,0:T(8,128)(2,1)S(1)} %bitcast.55, bf16[1,3,512,512]{3,2,1,0:T(8,128)(2,1)} %param.12), kind=kOutput, calls=%fused_computation.8 | convolution fusion | flops 1612972032 | bytes 7864332 | tf_op jit(solution)/shard_map/kij,kjm->kim/dot_general | solution.py:26
  59.5 13.1 %all-reduce = (f32[3]{0:T(128)S(1)}, f32[3]{0:T(128)S(1)}) all-reduce(f32[3]{0:T(128)S(1)} %get-tuple-element.6, f32[3]{0:T(128)S(1)} %multiply_reduce_fusion.1), channel_id=1, replica_groups=mesh['dp'=32,'mp'=8] {'mp'}, use_global_device_ids=true, to_apply=%region_3.5 | all-reduce | flops 6 | bytes 48 | tf_op jit(solution)/shard_map/psum | solution.py:46
  72.6 2.4 %fusion.2 = bf16[1,3,512,512]{3,2,1,0:T(8,128)(2,1)S(1)} fusion(f32[3,512,512]{2,1,0:T(8,128)} %get-tuple-element.7, f32[3]{0:T(128)S(1)} %sqrt_negate_fusion), kind=kLoop, calls=%fused_computation.11 | loop fusion | flops 1572864 | bytes 4718604 | tf_op jit(solution)/shard_map/broadcast_in_dim | solution.py:48
  75.0 2.6 %copy.29 = bf16[1,3,512,512]{3,1,0,2:T(4,128)(2,1)} copy(bf16[1,3,512,512]{3,2,1,0:T(8,128)(2,1)S(1)} %fusion.2) | data formatting | bytes 3145728 | tf_op jit(solution)/shard_map/broadcast_in_dim | solution.py:48
  77.6 7.1 %all-to-all-start.1 = ((bf16[1,3,512,512]{3,1,0,2:T(4,128)(2,1)}), bf16[1,3,512,512]{3,1,0,2:T(4,128)(2,1)}, u32[]{:S(2)}, u32[]{:S(2)}) async-start(bf16[1,3,512,512]{3,1,0,2:T(4,128)(2,1)} %copy.29), calls=%async_computation.1 | async-start | bytes 4194304 | tf_op jit(solution)/shard_map/all_to_all | solution.py:48
  84.7 0.9 scatter_custom_fusion
  85.6 0.0 copy-start.1
  85.6 3.8 %fusion.7 = bf16[1,3,512,512]{3,2,1,0:T(8,128)(2,1)} fusion(bf16[3,512,512]{2,1,0:T(8,128)(2,1)S(1)} %bitcast.56, bf16[1,3,512,512]{3,2,1,0:T(8,128)(2,1)} %param.11), kind=kOutput, calls=%fused_computation.18 | convolution fusion | flops 809238528 | bytes 4718592 | tf_op jit(solution)/shard_map/kji,kjm->kim/dot_general | solution.py:15
  89.4 0.0 copy-done.1
  89.4 2.2 %fusion.6 = bf16[1,3,512,512]{3,2,1,0:T(8,128)(2,1)} fusion(bf16[3,512,512]{2,1,0:T(8,128)(2,1)S(1)} %bitcast.57, bf16[1,3,512,512]{3,2,1,0:T(8,128)(2,1)S(1)} %copy-done.1), kind=kOutput, calls=%fused_computation.17 | convolution fusion | flops 809238528 | bytes 4718592 | tf_op jit(solution)/shard_map/kij,kmj->kim/dot_general | solution.py:12
  91.6 41.2 %all-to-all-done.1 = bf16[1,3,512,512]{3,1,0,2:T(4,128)(2,1)} async-done(((bf16[1,3,512,512]{3,1,0,2:T(4,128)(2,1)}), bf16[1,3,512,512]{3,1,0,2:T(4,128)(2,1)}, u32[]{:S(2)}, u32[]{:S(2)}) %all-to-all-start.1) | async-done | bytes 1572896 | tf_op jit(solution)/shard_map/all_to_all | solution.py:48
  132.8 2.0 %copy.30 = bf16[1,3,512,512]{3,2,1,0:T(8,128)(2,1)S(1)} copy(bf16[1,3,512,512]{3,1,0,2:T(4,128)(2,1)} %all-to-all-done.1) | data formatting | bytes 3145728 | tf_op jit(solution)/shard_map/all_to_all | solution.py:48
  134.8 0.1 copy.31
  134.9 1.9 %gather_fusion.1 = bf16[96,16,512]{2,1,0:T(8,128)(2,1)} fusion(bf16[96,16,512]{2,1,0:T(8,128)(2,1)S(1)} %bitcast.54, s32[1024]{0:T(1024)S(1)} %pad_clamp_fusion), kind=kCustom, calls=%fused_computation.1.clone | custom fusion | bytes 3146112 | tf_op jit(solution)/shard_map/jit(_take)/gather | solution.py:54
  136.8 2.8 %bitcast_select_fusion = bf16[1,96,16,512]{3,2,1,0:T(8,128)(2,1)} fusion(bf16[96,16,512]{2,1,0:T(8,128)(2,1)} %gather_fusion.1, pred[96]{0:T(512)(128)(4,1)S(1)} %compare_and_fusion), kind=kLoop, calls=%fused_computation.12 | loop fusion | flops 786432 | bytes 3145824 | tf_op jit(solution)/shard_map/jit(_take)/select_n | solution.py:54
  (6 shorter events, 0.0 us)
Async XLA Ops:
  0.6 1.5 %copy-start = (bf16[1,96,16,512]{3,2,1,0:T(8,128)(2,1)S(1)}, bf16[1,96,16,512]{3,2,1,0:T(8,128)(2,1)}, u32[]{:S(2)}) copy-start(bf16[1,96,16,512]{3,2,1,0:T(8,128)(2,1)} %param.8) | copy-start | bytes 4718596
  77.6 55.2 %all-to-all-start.1 = ((bf16[1,3,512,512]{3,1,0,2:T(4,128)(2,1)}), bf16[1,3,512,512]{3,1,0,2:T(4,128)(2,1)}, u32[]{:S(2)}, u32[]{:S(2)}) async-start(bf16[1,3,512,512]{3,1,0,2:T(4,128)(2,1)} %copy.29), calls=%async_computation.1 | async-start | bytes 4194304 | tf_op jit(solution)/shard_map/all_to_all | solution.py:48
  85.6 3.8 %copy-start.1 = (bf16[1,3,512,512]{3,2,1,0:T(8,128)(2,1)S(1)}, bf16[1,3,512,512]{3,2,1,0:T(8,128)(2,1)}, u32[]{:S(2)}) copy-start(bf16[1,3,512,512]{3,2,1,0:T(8,128)(2,1)} %param.10) | copy-start | bytes 4718596
where the time goes:
time: 141 us; the launch traced here: 140 us
  blocking collectives  63.4 us (45%)
  waiting for transfers between devices  41.2 us (29%)
  matrix products  11.5 us (8%)
  local copies, waits for them, and re-layouts  8.36 us (6%)
  other arithmetic  7.32 us (5%)
  starting transfers between devices  7.06 us (5%)
    all_to_all x1, blocking collectives, body(): lax.all_to_all(ordered, 'dp', split_axis=1, concat_axis=2, tiled=True)[0]  50.3 us
    all_to_all x1, waiting for transfers between devices, body(): lax.all_to_all(update_slot[None], 'dp', split_axis=2, concat_axis=1, tile...  41.2 us
    psum x1, blocking collectives, body(): grad_total, cond_total = lax.psum((grad_square, cond_square), 'mp')  13.1 us
    all_to_all x1, starting transfers between devices, body(): lax.all_to_all(update_slot[None], 'dp', split_axis=2, concat_axis=1, tile...  7.06 us
    dot_general x1, matrix products, local_blocks(): jnp.einsum('kij,kjm->kim', left_applied, right_inv, preferred_element_typ...  5.54 us
    dot_general x1, matrix products, local_blocks(): jnp.einsum('kji,kjm->kim', grad_block, grad_block, preferred_element_type...  3.77 us
  transfers between devices with their start and end apart: 1, of which 1 were waited for; matrix products, arithmetic and copies ran while one was open for 5% of the time, Pallas kernels for 0%

commit v1 on v0

v1 whole, which is shorter than its diff:
```python
import functools

import jax
import jax.numpy as jnp
from jax import lax
from jax.experimental import pallas as pl
from jax.experimental.pallas import tpu as pltpu
from jax.sharding import PartitionSpec as P

MESH = pl.DeviceIdType.MESH
factor_decay = 0.9
epsilon = 1e-06


def exchange_kernel(
    sizes,
    grad,
    order,
    left_old,
    right_old,
    left_inv,
    right_inv,
    returned,
    left_new,
    right_new,
    strips,
    stage,
    owned,
    lf,
    rf,
    lr,
    rr,
    cond,
    update,
    sums_out,
    sums_in,
    load_sem,
    out_send,
    out_recv,
    sum_send,
    sum_recv,
    back_send,
    back_recv,
):
    n_dp, n_mp, per, rows = sizes
    blocks = n_dp * per
    size = owned.shape[-1]
    dp = lax.axis_index("dp")
    mp = lax.axis_index("mp")
    coef = (1.0 - factor_decay) / size

    loads = [
        pltpu.make_async_copy(src, dst, load_sem.at[i])
        for i, (src, dst) in enumerate(
            (
                (grad.at[0], strips),
                (left_inv.at[0], lr),
                (right_inv.at[0], rr),
                (left_old.at[0], lf),
                (right_old.at[0], rf),
            )
        )
    ]
    loads[0].start()

    barrier = pltpu.get_barrier_semaphore()

    @pl.loop(1, n_dp)
    def _(j):
        pl.semaphore_signal(
            barrier, inc=1, device_id=(lax.rem(dp + j, n_dp), mp), device_id_type=MESH
        )

    @pl.loop(1, n_mp)
    def _(j):
        pl.semaphore_signal(
            barrier, inc=1, device_id=(dp, lax.rem(mp + j, n_mp)), device_id_type=MESH
        )

    for load in loads[1:]:
        load.start()
    loads[0].wait()

    @pl.loop(0, blocks)
    def _(p):
        stage[p] = strips[order[p]]

    my_rows = pl.ds(pl.multiple_of(dp * rows, rows), rows)
    for k in range(per):
        owned[k, my_rows, :] = stage[dp * per + k]

    pl.semaphore_wait(barrier, n_dp - 1 + n_mp - 1)

    @pl.loop(0, per)
    def _(k):
        @pl.loop(1, n_dp)
        def _(j):
            dst = lax.rem(dp + j, n_dp)
            pltpu.make_async_remote_copy(
                src_ref=stage.at[dst * per + k],
                dst_ref=owned.at[k, my_rows],
                send_sem=out_send,
                recv_sem=out_recv.at[k],
                device_id=(dst, mp),
                device_id_type=MESH,
            ).start()

    for load in loads[1:]:
        load.wait()

    @pl.loop(0, per)
    def _(k):
        others = owned.at[k, pl.ds(0, (n_dp - 1) * rows)]
        pltpu.make_async_copy(others, others, out_recv.at[k]).wait()

        applied = jnp.dot(lr[k], owned[k], preferred_element_type=jnp.float32).astype(jnp.bfloat16)
        cond[...] = jnp.dot(applied, rr[k], preferred_element_type=jnp.float32)
        wide = owned[k].astype(jnp.float32)
        grad_square = jnp.sum(wide * wide)
        cond_square = jnp.sum(cond[...] * cond[...])
        row = lax.broadcasted_iota(jnp.int32, (8, 128), 0)
        mine = jnp.where(row == 0, grad_square, cond_square)
        sums_out[k] = mine
        sums_in[k, mp] = mine

        @pl.loop(1, n_mp)
        def _(j):
            pltpu.make_async_remote_copy(
                src_ref=sums_out.at[k],
                dst_ref=sums_in.at[k, mp],
                send_sem=sum_send,
                recv_sem=sum_recv.at[k],
                device_id=(dp, lax.rem(mp + j, n_mp)),
                device_id_type=MESH,
            ).start()

        block = owned[k]
        gram_left = lax.dot_general(
            block, block, (((1,), (1,)), ((), ())), preferred_element_type=jnp.float32
        )
        left_new[k] = (factor_decay * lf[k].astype(jnp.float32) + coef * gram_left).astype(
            jnp.bfloat16
        )
        gram_right = lax.dot_general(
            block, block, (((0,), (0,)), ((), ())), preferred_element_type=jnp.float32
        )
        right_new[k] = (factor_decay * rf[k].astype(jnp.float32) + coef * gram_right).astype(
            jnp.bfloat16
        )

        parts = sums_in.at[k, pl.ds(0, n_mp - 1)]
        pltpu.make_async_copy(parts, parts, sum_recv.at[k]).wait()
        total = jnp.sum(sums_in[k], axis=0)
        graft = jnp.sqrt((total[0:1, 0:1] + epsilon) / (total[1:2, 0:1] + epsilon))
        update[k] = (-graft * cond[...]).astype(jnp.bfloat16)
        returned[dp * per + k] = update[k, my_rows, :]

        @pl.loop(1, n_dp)
        def _(j):
            dst = lax.rem(dp + j, n_dp)
            pltpu.make_async_remote_copy(
                src_ref=update.at[k, pl.ds(pl.multiple_of(dst * rows, rows), rows)],
                dst_ref=returned.at[dp * per + k],
                send_sem=back_send,
                recv_sem=back_recv,
                device_id=(dst, mp),
                device_id_type=MESH,
            ).start()

    others = (n_dp - 1) * per
    for sem in (out_send, back_send):
        pltpu.make_async_copy(
            stage.at[pl.ds(0, others)], stage.at[pl.ds(0, others)], sem
        ).wait()
    for k in range(per):
        parts = sums_in.at[k, pl.ds(0, n_mp - 1)]
        pltpu.make_async_copy(parts, parts, sum_send).wait()
    arrived = returned.at[pl.ds(0, others)]
    pltpu.make_async_copy(arrived, arrived, back_recv).wait()


def finish_kernel(order, returned, left, right, update, left_next, right_next, placed, sem):
    copies = [
        pltpu.make_async_copy(left, left_next.at[0], sem.at[0]),
        pltpu.make_async_copy(right, right_next.at[0], sem.at[1]),
        pltpu.make_async_copy(placed, update.at[0], sem.at[2]),
    ]
    copies[0].start()
    copies[1].start()

    @pl.loop(0, placed.shape[0])
    def _(p):
        placed[order[p]] = returned[p]

    copies[2].start()
    for copy in copies:
        copy.wait()


def body(n_dp, n_mp, gradient, owner_order, left_factor, right_factor, left_root, right_root):
    _, blocks, rows, size = gradient.shape
    per = left_factor.shape[1]
    bf16, f32 = jnp.bfloat16, jnp.float32
    strips = (blocks, rows, size)
    squares = (per, size, size)
    any_spec = pl.BlockSpec(memory_space=pl.ANY)
    smem_spec = pl.BlockSpec(memory_space=pltpu.SMEM)
    vmem_spec = pl.BlockSpec(memory_space=pltpu.VMEM)
    far = lambda x: pltpu.with_memory_space_constraint(x, pltpu.HBM)
    macs = 4 * per * size**3
    moved = gradient.size * 2
    returned, left_new, right_new = pl.pallas_call(
        functools.partial(exchange_kernel, (n_dp, n_mp, per, rows)),
        out_shape=[
            pltpu.VMEM(strips, bf16),
            pltpu.VMEM(squares, bf16),
            pltpu.VMEM(squares, bf16),
        ],
        in_specs=[any_spec, smem_spec] + [any_spec] * 4,
        out_specs=[vmem_spec] * 3,
        scratch_shapes=[
            pltpu.VMEM(strips, bf16),
            pltpu.VMEM(strips, bf16),
            pltpu.VMEM(squares, bf16),
            pltpu.VMEM(squares, bf16),
            pltpu.VMEM(squares, bf16),
            pltpu.VMEM(squares, bf16),
            pltpu.VMEM(squares, bf16),
            pltpu.VMEM((size, size), f32),
            pltpu.VMEM(squares, bf16),
            pltpu.VMEM((per, 8, 128), f32),
            pltpu.VMEM((per, n_mp, 8, 128), f32),
            pltpu.SemaphoreType.DMA((5,)),
            pltpu.SemaphoreType.DMA(()),
            pltpu.SemaphoreType.DMA((per,)),
            pltpu.SemaphoreType.DMA(()),
            pltpu.SemaphoreType.DMA((per,)),
            pltpu.SemaphoreType.DMA(()),
            pltpu.SemaphoreType.DMA(()),
        ],
        compiler_params=pltpu.CompilerParams(
            collective_id=0, has_side_effects=True, vmem_limit_bytes=40 << 20
        ),
        cost_estimate=pl.CostEstimate(
            flops=2 * macs, bytes_accessed=8 * moved, transcendentals=0
        ),
        name="exchange",
    )(
        far(gradient),
        owner_order,
        far(left_factor),
        far(right_factor),
        far(left_root),
        far(right_root),
    )

    keep = lambda x: pltpu.with_memory_space_constraint(x, pltpu.VMEM)
    return pl.pallas_call(
        finish_kernel,
        out_shape=[
            jax.ShapeDtypeStruct(gradient.shape, bf16),
            jax.ShapeDtypeStruct((1,) + squares, bf16),
            jax.ShapeDtypeStruct((1,) + squares, bf16),
        ],
        in_specs=[smem_spec] + [vmem_spec] * 3,
        out_specs=[any_spec] * 3,
        scratch_shapes=[pltpu.VMEM(strips, bf16), pltpu.SemaphoreType.DMA((3,))],
        compiler_params=pltpu.CompilerParams(vmem_limit_bytes=16 << 20),
        cost_estimate=pl.CostEstimate(flops=0, bytes_accessed=6 * moved, transcendentals=0),
        name="finish",
    )(owner_order, keep(returned), keep(left_new), keep(right_new))


def solution(mesh):
    return jax.shard_map(
        functools.partial(body, mesh.shape["dp"], mesh.shape["mp"]),
        mesh=mesh,
        in_specs=(
            P("mp", None, "dp", None),
            P(),
            P("mp", "dp", None, None),
            P("mp", "dp", None, None),
            P("mp", "dp", None, None),
            P("mp", "dp", None, None),
        ),
        out_specs=(P("mp", None, "dp", None), P("mp", "dp", None, None), P("mp", "dp", None, None)),
        check_vma=False,
    )
```

time: 141 us -> 83.7 us (0.59)
  Pallas kernels: 0 us -> 81.1 us
  blocking collectives: 63.4 us -> 0 us
  waiting for transfers between devices: 41.2 us -> 0 us
  matrix products: 11.5 us -> 0 us
  local copies, waits for them, and re-layouts: 8.36 us -> 0.65 us
  other arithmetic: 7.32 us -> 0 us
  starting transfers between devices: 7.06 us -> 0 us
    pallas_call x0 -> x2, Pallas kernels: none -> 81.1 us  [the longest x1 78.3 us: body(): pl.pallas_call(functools.partial(exchange_kernel, (n_dp, n_mp, per, rows)...]
    all_to_all x1 -> x0, blocking collectives: 50.3 us -> none  [body(): lax.all_to_all(ordered, 'dp', split_axis=1, concat_axis=2, tiled=True)[0]]
    all_to_all x1 -> x0, waiting for transfers between devices: 41.2 us -> none  [body(): lax.all_to_all(update_slot[None], 'dp', split_axis=2, concat_axis=1, tile...]
    psum x1 -> x0, blocking collectives: 13.1 us -> none  [body(): grad_total, cond_total = lax.psum((grad_square, cond_square), 'mp')]
    dot_general x3 -> x0, matrix products: 11.5 us -> none  [the longest x1 5.54 us: local_blocks(): jnp.einsum('kij,kjm->kim', left_applied, right_inv, preferred_element_typ...]
    all_to_all x1 -> x0, starting transfers between devices: 7.06 us -> none  [body(): lax.all_to_all(update_slot[None], 'dp', split_axis=2, concat_axis=1, tile...]
    select_n x4 -> x0, other arithmetic: 3.77 us -> none  [the longest x2 2.77 us: body(): update = jnp.take(returned, places, axis=1)]
    broadcast_in_dim x1 -> x0, local copies, waits for them, and re-layouts: 2.64 us -> none  [body(): update_slot[None]]
  transfers between devices with their start and end apart: 1 -> 0, of which waited for: 1 -> 0; matrix products, arithmetic and copies ran while one was open for 5% -> 0% of each run, Pallas kernels for 0% -> 0%
where the time goes in v1:
time: 83.7 us; the launch traced here: 82.4 us
  Pallas kernels  81.1 us (97%)
    pallas_call x1, Pallas kernels, body(): pl.pallas_call(functools.partial(exchange_kernel, (n_dp, n_mp, per, rows)...  78.3 us
    pallas_call x1, Pallas kernels, body(): pl.pallas_call(finish_kernel, out_shape=[jax.ShapeDtypeStruct(gradient.sh...  2.75 us

profile of v1, /device:TPU:40, one launch (start us, length us, event | category | flops | bytes accessed | tf_op | source)
XLA Modules:
  0.0 82.4 jit_solution(7493179849030061225)
XLA Ops:
  0.6 0.0 copy-start
  0.6 0.6 copy-done
  1.3 78.3 %exchange.1 = (bf16[96,16,512]{2,1,0:T(8,128)(2,1)S(1)}, bf16[3,512,512]{2,1,0:T(8,128)(2,1)S(1)}, bf16[3,512,512]{2,1,0:T(8,128)(2,1)S(1)}) custom-call(bf16[1,96,16,512]{3,2,1,0:T(8,128)(2,1)} %grad.1, s32[96]{0:T(128)S(1)} %copy-done, bf16[1,3,512,512]{3,2,1,0:T(8,128)(2,1)} %left_old.1, bf16[1,3,512,512]{3,2,1,0:T(8,128)(2,1)} %right_old.1, ...), custom_call_target="tpu_custom_call" | custom-call | flops 3221225472 | bytes 12582912 | tf_op jit(solution)/shard_map/exchange/pallas_call | solution.py:212
  79.6 2.7 %finish.1 = (bf16[1,96,16,512]{3,2,1,0:T(8,128)(2,1)}, bf16[1,3,512,512]{3,2,1,0:T(8,128)(2,1)}, bf16[1,3,512,512]{3,2,1,0:T(8,128)(2,1)}) custom-call(s32[96]{0:T(128)S(1)} %copy-done, bf16[96,16,512]{2,1,0:T(8,128)(2,1)S(1)} %get-tuple-element.6.returned, bf16[3,512,512]{2,1,0:T(8,128)(2,1)S(1)} %get-tuple-element.7.left, ...), custom_call_target="tpu_custom_call" | custom-call | bytes 9437184 | tf_op jit(solution)/shard_map/finish/pallas_call | solution.py:258
Async XLA Ops:
  0.6 0.7 copy-start

commit v2 on v1

v2 whole, which is shorter than its diff:
```python
import functools

import jax
import jax.numpy as jnp
from jax import lax
from jax.experimental import pallas as pl
from jax.experimental.pallas import tpu as pltpu
from jax.sharding import PartitionSpec as P

MESH = pl.DeviceIdType.MESH
factor_decay = 0.9
epsilon = 1e-06
RING = 8


def exchange_kernel(
    sizes,
    grad,
    order,
    left_old,
    right_old,
    left_inv,
    right_inv,
    returned,
    left_new,
    right_new,
    strips,
    stage,
    owned,
    slots,
    lf,
    rf,
    lr,
    rr,
    cond,
    update,
    sums_out,
    sums_in,
    news,
    load_sem,
    out_send,
    out_recv,
    sum_send,
    sum_recv,
    back_send,
    back_recv,
):
    n_dp, per, rows = sizes
    n_y, n_z = n_dp // RING, RING
    blocks = n_dp * per
    size = owned.shape[-1]
    dp = lax.axis_index("dp")
    mp = lax.axis_index("mp")
    coef = (1.0 - factor_decay) / size
    y, z = dp // n_z, lax.rem(dp, n_z)
    x, core = mp // 2, lax.rem(mp, 2)
    partners = (2 * x + 1 - core, 2 * (x + 1 - 2 * lax.rem(x, 2)) + core, 2 * (3 - x) + core)

    def peer(dy, dz):
        return lax.rem(y + dy, n_y) * n_z + lax.rem(z + dz, n_z)

    loads = [
        pltpu.make_async_copy(src, dst, load_sem.at[i])
        for i, (src, dst) in enumerate(
            (
                (order, slots),
                (grad.at[0], strips),
                (left_inv.at[0], lr),
                (right_inv.at[0], rr),
                (left_old.at[0], lf),
                (right_old.at[0], rf),
            )
        )
    ]
    loads[0].start()
    loads[1].start()

    barrier = pltpu.get_barrier_semaphore()

    def signal(sem, dev):
        pl.semaphore_signal(sem, inc=1, device_id=dev, device_id_type=MESH)

    for dy in (2, 1, n_y - 1):
        signal(barrier, (peer(dy, 0), mp))
    for dz in (1, n_z - 1):
        signal(barrier, (peer(0, dz), mp))
    for partner in partners:
        signal(barrier, (dp, partner))

    for load in loads[2:]:
        load.start()
    loads[0].wait()
    loads[1].wait()

    my_rows = pl.ds(pl.multiple_of(dp * rows, rows), rows)

    def gather(k):
        @pl.loop(0, n_dp, unroll=4)
        def _(d):
            stage[d * per + k] = strips[slots[d * per + k]]

        owned[k, my_rows, :] = stage[dp * per + k]

    def send(k, dst):
        pltpu.make_async_remote_copy(
            src_ref=stage.at[dst * per + k],
            dst_ref=owned.at[k, my_rows],
            send_sem=out_send,
            recv_sem=out_recv.at[k],
            device_id=(dst, mp),
            device_id_type=MESH,
        ).start()

    def send_near(k):
        for dz in (1, n_z - 1):
            send(k, peer(0, dz))
        for dy in range(1, n_y):
            send(k, peer(dy, 0))

    def relay(step):
        for dz in (1, n_z - 1):
            signal(news.at[step], (peer(0, dz), mp))

    gather(0)
    pl.semaphore_wait(barrier, n_y - 1 + 2 + len(partners))
    relay(0)
    send_near(0)
    for k in range(1, per):
        gather(k)
        send_near(k)
    for step in range(n_z // 2):
        pl.semaphore_wait(news.at[step], 2)
        if step + 1 < n_z // 2:
            relay(step + 1)
        dist = step + 1
        sides = (dist, n_z - dist) if 2 * dist < n_z else (dist,)
        for dz in sides:

            @pl.loop(1, n_y)
            def _(dy):
                send(0, peer(dy, dz))

        if dist + 1 <= n_z // 2:
            for dz in (dist + 1, n_z - dist - 1)[: 2 if 2 * dist + 2 < n_z else 1]:
                send(0, peer(0, dz))

    for k in range(1, per):

        @pl.loop(2, n_z - 1)
        def _(dz):
            send(k, peer(0, dz))

        @pl.loop(0, (n_y - 1) * (n_z - 1))
        def _(i):
            send(k, peer(1 + i // (n_z - 1), 1 + lax.rem(i, n_z - 1)))

    for load in loads[2:]:
        load.wait()

    @pl.loop(0, per)
    def _(k):
        others = owned.at[k, pl.ds(0, (n_dp - 1) * rows)]
        pltpu.make_async_copy(others, others, out_recv.at[k]).wait()

        applied = jnp.dot(lr[k], owned[k], preferred_element_type=jnp.float32).astype(jnp.bfloat16)
        cond[...] = jnp.dot(applied, rr[k], preferred_element_type=jnp.float32)
        wide = owned[k].astype(jnp.float32)
        grad_square = jnp.sum(wide * wide)
        cond_square = jnp.sum(cond[...] * cond[...])
        row = lax.broadcasted_iota(jnp.int32, (8, 128), 0)
        mine = jnp.where(row == 0, grad_square, cond_square)
        def trade(step, value):
            sums_out[k, step] = value
            copy = pltpu.make_async_remote_copy(
                src_ref=sums_out.at[k, step],
                dst_ref=sums_in.at[k, step],
                send_sem=sum_send.at[k, step],
                recv_sem=sum_recv.at[k, step],
                device_id=(dp, partners[step]),
                device_id_type=MESH,
            )
            copy.start()
            return copy

        copy = trade(0, mine)

        block = owned[k]
        gram_left = lax.dot_general(
            block, block, (((1,), (1,)), ((), ())), preferred_element_type=jnp.float32
        )
        left_new[k] = (factor_decay * lf[k].astype(jnp.float32) + coef * gram_left).astype(
            jnp.bfloat16
        )
        gram_right = lax.dot_general(
            block, block, (((0,), (0,)), ((), ())), preferred_element_type=jnp.float32
        )
        right_new[k] = (factor_decay * rf[k].astype(jnp.float32) + coef * gram_right).astype(
            jnp.bfloat16
        )

        for step in range(len(partners)):
            copy.wait()
            total = sums_out[k, step] + sums_in[k, step]
            if step + 1 < len(partners):
                copy = trade(step + 1, total)
        graft = jnp.sqrt((total[0:1, 0:1] + epsilon) / (total[1:2, 0:1] + epsilon))
        update[k] = (-graft * cond[...]).astype(jnp.bfloat16)
        returned[dp * per + k] = update[k, my_rows, :]

        @pl.loop(1, n_dp)
        def _(j):
            dst = lax.rem(dp + j, n_dp)
            pltpu.make_async_remote_copy(
                src_ref=update.at[k, pl.ds(pl.multiple_of(dst * rows, rows), rows)],
                dst_ref=returned.at[dp * per + k],
                send_sem=back_send,
                recv_sem=back_recv,
                device_id=(dst, mp),
                device_id_type=MESH,
            ).start()

    others = (n_dp - 1) * per
    for sem in (out_send, back_send):
        pltpu.make_async_copy(
            stage.at[pl.ds(0, others)], stage.at[pl.ds(0, others)], sem
        ).wait()
    arrived = returned.at[pl.ds(0, others)]
    pltpu.make_async_copy(arrived, arrived, back_recv).wait()


def finish_kernel(
    order, returned, left, right, update, left_next, right_next, slots, placed, sem
):
    copies = [
        pltpu.make_async_copy(order, slots, sem.at[0]),
        pltpu.make_async_copy(left, left_next.at[0], sem.at[1]),
        pltpu.make_async_copy(right, right_next.at[0], sem.at[2]),
        pltpu.make_async_copy(placed, update.at[0], sem.at[3]),
    ]
    for copy in copies[:3]:
        copy.start()
    copies[0].wait()

    @pl.loop(0, placed.shape[0], unroll=4)
    def _(p):
        placed[slots[p]] = returned[p]

    copies[3].start()
    for copy in copies[1:]:
        copy.wait()


def body(n_dp, gradient, owner_order, left_factor, right_factor, left_root, right_root):
    _, blocks, rows, size = gradient.shape
    per = left_factor.shape[1]
    bf16, f32 = jnp.bfloat16, jnp.float32
    strips = (blocks, rows, size)
    squares = (per, size, size)
    any_spec = pl.BlockSpec(memory_space=pl.ANY)
    vmem_spec = pl.BlockSpec(memory_space=pltpu.VMEM)
    far = lambda x: pltpu.with_memory_space_constraint(x, pltpu.HBM)
    macs = 4 * per * size**3
    moved = gradient.size * 2
    returned, left_new, right_new = pl.pallas_call(
        functools.partial(exchange_kernel, (n_dp, per, rows)),
        out_shape=[
            pltpu.VMEM(strips, bf16),
            pltpu.VMEM(squares, bf16),
            pltpu.VMEM(squares, bf16),
        ],
        in_specs=[any_spec] * 6,
        out_specs=[vmem_spec] * 3,
        scratch_shapes=[
            pltpu.VMEM(strips, bf16),
            pltpu.VMEM(strips, bf16),
            pltpu.VMEM(squares, bf16),
            pltpu.SMEM((blocks,), jnp.int32),
            pltpu.VMEM(squares, bf16),
            pltpu.VMEM(squares, bf16),
            pltpu.VMEM(squares, bf16),
            pltpu.VMEM(squares, bf16),
            pltpu.VMEM((size, size), f32),
            pltpu.VMEM(squares, bf16),
            pltpu.VMEM((per, 3, 8, 128), f32),
            pltpu.VMEM((per, 3, 8, 128), f32),
            pltpu.SemaphoreType.REGULAR((RING // 2,)),
            pltpu.SemaphoreType.DMA((6,)),
            pltpu.SemaphoreType.DMA(()),
            pltpu.SemaphoreType.DMA((per,)),
            pltpu.SemaphoreType.DMA((per, 3)),
            pltpu.SemaphoreType.DMA((per, 3)),
            pltpu.SemaphoreType.DMA(()),
            pltpu.SemaphoreType.DMA(()),
        ],
        compiler_params=pltpu.CompilerParams(
            collective_id=0, has_side_effects=True, vmem_limit_bytes=40 << 20
        ),
        cost_estimate=pl.CostEstimate(
            flops=2 * macs, bytes_accessed=8 * moved, transcendentals=0
        ),
        name="exchange",
    )(
        far(gradient),
        far(owner_order),
        far(left_factor),
        far(right_factor),
        far(left_root),
        far(right_root),
    )

    keep = lambda x: pltpu.with_memory_space_constraint(x, pltpu.VMEM)
    return pl.pallas_call(
        finish_kernel,
        out_shape=[
            jax.ShapeDtypeStruct(gradient.shape, bf16),
            jax.ShapeDtypeStruct((1,) + squares, bf16),
            jax.ShapeDtypeStruct((1,) + squares, bf16),
        ],
        in_specs=[any_spec] + [vmem_spec] * 3,
        out_specs=[any_spec] * 3,
        scratch_shapes=[
            pltpu.SMEM((blocks,), jnp.int32),
            pltpu.VMEM(strips, bf16),
            pltpu.SemaphoreType.DMA((4,)),
        ],
        compiler_params=pltpu.CompilerParams(vmem_limit_bytes=16 << 20),
        cost_estimate=pl.CostEstimate(flops=0, bytes_accessed=6 * moved, transcendentals=0),
        name="finish",
    )(far(owner_order), keep(returned), keep(left_new), keep(right_new))


def solution(mesh):
    return jax.shard_map(
        functools.partial(body, mesh.shape["dp"]),
        mesh=mesh,
        in_specs=(
            P("mp", None, "dp", None),
            P(),
            P("mp", "dp", None, None),
            P("mp", "dp", None, None),
            P("mp", "dp", None, None),
            P("mp", "dp", None, None),
        ),
        out_specs=(P("mp", None, "dp", None), P("mp", "dp", None, None), P("mp", "dp", None, None)),
        check_vma=False,
    )
```

time: 83.7 us -> 81.1 us (0.969)
  Pallas kernels: 81.1 us -> 79 us
    pallas_call x1, Pallas kernels: 78.3 us -> 76.8 us  [body(): pl.pallas_call(functools.partial(exchange_kernel, (n_dp, per, rows)), out...]
where the time goes in v2:
time: 81.1 us; the launch traced here: 79.7 us
  Pallas kernels  79 us (97%)
    pallas_call x1, Pallas kernels, body(): pl.pallas_call(functools.partial(exchange_kernel, (n_dp, per, rows)), out...  76.8 us
    pallas_call x1, Pallas kernels, body(): pl.pallas_call(finish_kernel, out_shape=[jax.ShapeDtypeStruct(gradient.sh...  2.22 us

profile of v2, /device:TPU:40, one launch (start us, length us, event | category | flops | bytes accessed | tf_op | source)
XLA Modules:
  0.0 79.7 jit_solution(600207722581093669)
XLA Ops:
  0.6 76.8 %exchange.1 = (bf16[96,16,512]{2,1,0:T(8,128)(2,1)S(1)}, bf16[3,512,512]{2,1,0:T(8,128)(2,1)S(1)}, bf16[3,512,512]{2,1,0:T(8,128)(2,1)S(1)}) custom-call(bf16[1,96,16,512]{3,2,1,0:T(8,128)(2,1)} %grad.1, s32[96]{0:T(128)} %order.3, bf16[1,3,512,512]{3,2,1,0:T(8,128)(2,1)} %left_old.1, bf16[1,3,512,512]{3,2,1,0:T(8,128)(2,1)} %right_old.1, ...), custom_call_target="tpu_custom_call" | custom-call | flops 3221225472 | bytes 12582912 | tf_op jit(solution)/shard_map/exchange/pallas_call | solution.py:264
  77.4 2.2 %finish.1 = (bf16[1,96,16,512]{3,2,1,0:T(8,128)(2,1)}, bf16[1,3,512,512]{3,2,1,0:T(8,128)(2,1)}, bf16[1,3,512,512]{3,2,1,0:T(8,128)(2,1)}) custom-call(s32[96]{0:T(128)} %order.3, bf16[96,16,512]{2,1,0:T(8,128)(2,1)S(1)} %get-tuple-element.6.returned, bf16[3,512,512]{2,1,0:T(8,128)(2,1)S(1)} %get-tuple-element.7.left, ...), custom_call_target="tpu_custom_call" | custom-call | bytes 9437184 | tf_op jit(solution)/shard_map/finish/pallas_call | solution.py:312

commit v3 on v2

--- a/solution.py
+++ b/solution.py
@@ -11,6 +11,7 @@
 factor_decay = 0.9
 epsilon = 1e-06
 RING = 8
+EARLY = 3
 
 
 def exchange_kernel(
@@ -207,9 +208,7 @@
         update[k] = (-graft * cond[...]).astype(jnp.bfloat16)
         returned[dp * per + k] = update[k, my_rows, :]
 
-        @pl.loop(1, n_dp)
-        def _(j):
-            dst = lax.rem(dp + j, n_dp)
+        def send_back(dst):
             pltpu.make_async_remote_copy(
                 src_ref=update.at[k, pl.ds(pl.multiple_of(dst * rows, rows), rows)],
                 dst_ref=returned.at[dp * per + k],
@@ -218,6 +217,20 @@
                 device_id=(dst, mp),
                 device_id_type=MESH,
             ).start()
+
+        for chosen in (
+            lambda yy, zz: (zz < EARLY) & (yy == 0),
+            lambda yy, zz: (zz < EARLY) & (yy != 0),
+            lambda yy, zz: zz >= EARLY,
+        ):
+
+            @pl.loop(1, n_dp)
+            def _(j):
+                dst = lax.rem(dp + j, n_dp)
+
+                @pl.when(chosen(dst // n_z, lax.rem(dst, n_z)))
+                def _():
+                    send_back(dst)
 
     others = (n_dp - 1) * per
     for sem in (out_send, back_send):

time: 81.1 us -> 80.1 us (0.988); the launches traced: 79.7 us -> 80 us
  no operation moved by 1% of the time
where the time goes in v3:
time: 80.1 us; the launch traced here: 80 us
  Pallas kernels  79.3 us (99%)
    pallas_call x1, Pallas kernels, body(): pl.pallas_call(functools.partial(exchange_kernel, (n_dp, per, rows)), out...  77.1 us
    pallas_call x1, Pallas kernels, body(): pl.pallas_call(finish_kernel, out_shape=[jax.ShapeDtypeStruct(gradient.sh...  2.22 us

profile of v3, /device:TPU:40, one launch (start us, length us, event | category | flops | bytes accessed | tf_op | source)
XLA Modules:
  0.0 80.0 jit_solution(16481076406090276966)
XLA Ops:
  0.6 77.1 %exchange.1 = (bf16[96,16,512]{2,1,0:T(8,128)(2,1)S(1)}, bf16[3,512,512]{2,1,0:T(8,128)(2,1)S(1)}, bf16[3,512,512]{2,1,0:T(8,128)(2,1)S(1)}) custom-call(bf16[1,96,16,512]{3,2,1,0:T(8,128)(2,1)} %grad.1, s32[96]{0:T(128)} %order.3, bf16[1,3,512,512]{3,2,1,0:T(8,128)(2,1)} %left_old.1, bf16[1,3,512,512]{3,2,1,0:T(8,128)(2,1)} %right_old.1, ...), custom_call_target="tpu_custom_call" | custom-call | flops 3221225472 | bytes 12582912 | tf_op jit(solution)/shard_map/exchange/pallas_call | solution.py:277
  77.7 2.2 %finish.1 = (bf16[1,96,16,512]{3,2,1,0:T(8,128)(2,1)}, bf16[1,3,512,512]{3,2,1,0:T(8,128)(2,1)}, bf16[1,3,512,512]{3,2,1,0:T(8,128)(2,1)}) custom-call(s32[96]{0:T(128)} %order.3, bf16[96,16,512]{2,1,0:T(8,128)(2,1)S(1)} %get-tuple-element.6.returned, bf16[3,512,512]{2,1,0:T(8,128)(2,1)S(1)} %get-tuple-element.7.left, ...), custom_call_target="tpu_custom_call" | custom-call | bytes 9437184 | tf_op jit(solution)/shard_map/finish/pallas_call | solution.py:325

commit v4 on v3

--- a/solution.py
+++ b/solution.py
@@ -221,7 +221,8 @@
         for chosen in (
             lambda yy, zz: (zz < EARLY) & (yy == 0),
             lambda yy, zz: (zz < EARLY) & (yy != 0),
-            lambda yy, zz: zz >= EARLY,
+            lambda yy, zz: (zz == EARLY) | (zz == n_z - 1),
+            lambda yy, zz: (zz > EARLY) & (zz < n_z - 1),
         ):
 
             @pl.loop(1, n_dp)

time: 80.1 us -> 79.8 us (level)
  no operation moved by 1% of the time
where the time goes in v4:
time: 79.8 us; the launch traced here: 79.5 us
  Pallas kernels  78.8 us (99%)
    pallas_call x1, Pallas kernels, body(): pl.pallas_call(functools.partial(exchange_kernel, (n_dp, per, rows)), out...  76.6 us
    pallas_call x1, Pallas kernels, body(): pl.pallas_call(finish_kernel, out_shape=[jax.ShapeDtypeStruct(gradient.sh...  2.22 us

profile of v4, /device:TPU:40, one launch (start us, length us, event | category | flops | bytes accessed | tf_op | source)
XLA Modules:
  0.0 79.5 jit_solution(11677390585430799743)
XLA Ops:
  0.6 76.6 %exchange.1 = (bf16[96,16,512]{2,1,0:T(8,128)(2,1)S(1)}, bf16[3,512,512]{2,1,0:T(8,128)(2,1)S(1)}, bf16[3,512,512]{2,1,0:T(8,128)(2,1)S(1)}) custom-call(bf16[1,96,16,512]{3,2,1,0:T(8,128)(2,1)} %grad.1, s32[96]{0:T(128)} %order.3, bf16[1,3,512,512]{3,2,1,0:T(8,128)(2,1)} %left_old.1, bf16[1,3,512,512]{3,2,1,0:T(8,128)(2,1)} %right_old.1, ...), custom_call_target="tpu_custom_call" | custom-call | flops 3221225472 | bytes 12582912 | tf_op jit(solution)/shard_map/exchange/pallas_call | solution.py:278
  77.3 2.2 %finish.1 = (bf16[1,96,16,512]{3,2,1,0:T(8,128)(2,1)}, bf16[1,3,512,512]{3,2,1,0:T(8,128)(2,1)}, bf16[1,3,512,512]{3,2,1,0:T(8,128)(2,1)}) custom-call(s32[96]{0:T(128)} %order.3, bf16[96,16,512]{2,1,0:T(8,128)(2,1)S(1)} %get-tuple-element.6.returned, bf16[3,512,512]{2,1,0:T(8,128)(2,1)S(1)} %get-tuple-element.7.left, ...), custom_call_target="tpu_custom_call" | custom-call | bytes 9437184 | tf_op jit(solution)/shard_map/finish/pallas_call | solution.py:326

commit v5 on v4

--- a/solution.py
+++ b/solution.py
@@ -88,8 +88,6 @@
     for partner in partners:
         signal(barrier, (dp, partner))
 
-    for load in loads[2:]:
-        load.start()
     loads[0].wait()
     loads[1].wait()
 
@@ -126,6 +124,8 @@
     pl.semaphore_wait(barrier, n_y - 1 + 2 + len(partners))
     relay(0)
     send_near(0)
+    for load in loads[2:]:
+        load.start()
     for k in range(1, per):
         gather(k)
         send_near(k)

time: 79.8 us -> 79.8 us (level)
  no operation moved by 1% of the time
where the time goes in v5:
time: 79.8 us; the launch traced here: 79.5 us
  Pallas kernels  78.8 us (99%)
    pallas_call x1, Pallas kernels, body(): pl.pallas_call(functools.partial(exchange_kernel, (n_dp, per, rows)), out...  76.6 us
    pallas_call x1, Pallas kernels, body(): pl.pallas_call(finish_kernel, out_shape=[jax.ShapeDtypeStruct(gradient.sh...  2.22 us

profile of v5, /device:TPU:40, one launch (start us, length us, event | category | flops | bytes accessed | tf_op | source)
XLA Modules:
  0.0 79.5 jit_solution(8060402115607052893)
XLA Ops:
  0.6 76.6 %exchange.1 = (bf16[96,16,512]{2,1,0:T(8,128)(2,1)S(1)}, bf16[3,512,512]{2,1,0:T(8,128)(2,1)S(1)}, bf16[3,512,512]{2,1,0:T(8,128)(2,1)S(1)}) custom-call(bf16[1,96,16,512]{3,2,1,0:T(8,128)(2,1)} %grad.1, s32[96]{0:T(128)} %order.3, bf16[1,3,512,512]{3,2,1,0:T(8,128)(2,1)} %left_old.1, bf16[1,3,512,512]{3,2,1,0:T(8,128)(2,1)} %right_old.1, ...), custom_call_target="tpu_custom_call" | custom-call | flops 3221225472 | bytes 12582912 | tf_op jit(solution)/shard_map/exchange/pallas_call | solution.py:278
  77.3 2.2 %finish.1 = (bf16[1,96,16,512]{3,2,1,0:T(8,128)(2,1)}, bf16[1,3,512,512]{3,2,1,0:T(8,128)(2,1)}, bf16[1,3,512,512]{3,2,1,0:T(8,128)(2,1)}) custom-call(s32[96]{0:T(128)} %order.3, bf16[96,16,512]{2,1,0:T(8,128)(2,1)S(1)} %get-tuple-element.6.returned, bf16[3,512,512]{2,1,0:T(8,128)(2,1)S(1)} %get-tuple-element.7.left, ...), custom_call_target="tpu_custom_call" | custom-call | bytes 9437184 | tf_op jit(solution)/shard_map/finish/pallas_call | solution.py:326
